TPU v7x, 32 devices: a whole 2x2x4 slice. The times are simulated.
32 devices in a mesh: groups: 2 (over y), rows: 4 (over z), sect: 4 (over x, core).
Axes of the slice: x: 2, y: 2, z: 4, core: 2. Of those that a mesh axis runs over, the one named last changes fastest.
Arguments:
- blocks: bfloat16 [128, 8, 256, 256], P(('rows', 'sect')), may hold values from -0.125 to 0.125
- col_index: int32 [128, 8], P(('rows', 'sect')), may hold values from 0 to 127, as said below
- counts: int32 [128], P(('rows', 'sect')), may hold values from 1 to 8, as said below
- shifts: float32 [4], P('groups'), parts along dimension 0, may hold values from 0.1 to 0.4
- vectors: float32 [64, 32768], P('groups', ('rows', 'sect')), parts along dimension 0, may hold values from -6 to 6
Outputs:
- krylov_block: float32 [64, 32768], P('groups', ('rows', 'sect')), parts along dimension 0
There are 2 independent parts, one for each index of `groups`. A program takes and returns all parts, laid end to end along the dimension named above; an argument that names none is the same for every part. Nothing has to cross between parts.
Inputs may be any that keep to these rules, and one draw needn't show every extreme that they name: `col_index`: slot 0 of block row i names i itself. Every slot of block row (r, s, k) names a block row whose r differs from r by at most one; a thermal row names only thermal block rows. Duplicates may occur. `counts`: each aligned group of 16 block rows holds a row with all 8 slots live.
All inputs are finite; a program needn't handle non-finite values.
Results may differ from a plain program's by a relative error of at most 0.013.
Values may be sent and summed in bfloat16 or wider, within the bound.
A program may use at most 64 MiB of HBM per device.

v0:
```python
import jax
import jax.numpy as jnp
from jax import lax
from jax.sharding import PartitionSpec as P

STEPS = 12


def padded(shard, sides, width):
    for axis, dim in sides:
        size, length = (lax.axis_size(axis), shard.shape[dim])
        up = [(i, (i + 1) % size) for i in range(size - 1)]
        down = [(j, i) for i, j in up]
        last = lax.slice_in_dim(shard, length - width, length, axis=dim)
        first = lax.slice_in_dim(shard, 0, width, axis=dim)
        before = lax.ppermute(last, axis, up)
        after = lax.ppermute(first, axis, down)
        shard = jnp.concatenate([before, shard, after], axis=dim)
    return shard


def per_device(blocks, col_index, counts, shifts, vectors):
    sections = lax.axis_size("sect")
    rblk = col_index.shape[0]
    slots = col_index.shape[1]
    width = blocks.shape[2]
    ncols = vectors.shape[0]
    range_here = lax.axis_index("rows")
    sect_here = lax.axis_index("sect")
    target_range = col_index // (sections * rblk)
    target_sect = col_index // rblk % sections
    target_loc = col_index % rblk
    offset = target_range - range_here + 1
    position = (offset * sections + target_sect) * rblk + target_loc
    position = position.reshape(-1)
    live = (
        (jnp.arange(slots, dtype=jnp.int32)[None, :] < counts[:, None])
        .astype(jnp.bfloat16)
        .reshape(-1)
    )
    shift_here = jnp.where(sect_here == 0, shifts[0], shifts[1])
    flat_blocks = blocks.reshape(rblk * slots, width, width)

    def advance(applied, current):
        narrow = current.astype(jnp.bfloat16)
        pieces = lax.all_gather(narrow, "sect", axis=1, tiled=True)
        window = padded(pieces, (("rows", 1),), sections * rblk * width)
        window = window.reshape(ncols, -1, width)
        chosen = jnp.take(window, position, axis=1) * live[None, :, None]
        products = jnp.einsum(
            "cqb,qab->cqa", chosen, flat_blocks, preferred_element_type=jnp.float32
        )
        summed = (
            products.reshape(ncols, rblk, slots, width).sum(axis=2).reshape(ncols, rblk * width)
        )
        return summed + shift_here * current

    return lax.fori_loop(0, STEPS, advance, vectors)


def solution(mesh):
    return jax.shard_map(
        per_device,
        mesh=mesh,
        in_specs=(
            P(("rows", "sect"), None, None, None),
            P(("rows", "sect"), None),
            P(("rows", "sect")),
            P("groups"),
            P("groups", ("rows", "sect")),
        ),
        out_specs=P("groups", ("rows", "sect")),
        check_vma=False,
    )
```

profile of v0, /device:TPU:1, one launch (start us, length us, event | category | flops | bytes accessed | tf_op | source)
XLA Modules:
  0.0 386.6 jit_solution(11987320421622677028)
XLA Ops:
  4.3 381.6 %while.11 = (s32[]{:T(128)}, f32[32,2048]{1,0:T(8,128)S(1)}, s32[64]{0:T(128)S(1)}, bf16[64,256,256]{2,1,0:T(8,128)(2,1)}, f32[]{:T(128)}, /*index=5*/s32[8]{0:T(128)}, s32[]{:T(128)}) while((s32[]{:T(128)}, f32[32,2048]{1,0:T(8,128)S(1)}, s32[64]{0:T(128)S(1)}, bf16[64,256,256]{2,1,0:T(8,128)(2,1)}, f32[]{:T(128)}, ...), condition=%wide.region_2.3_spmd.clone, body=%wide.region_0.2_spmd.clone.sunk | while | flops 274859712 | bytes 24647744 | solution.py:58
  4.3 8.5 %all_gather.5 = bf16[32,8192]{1,0:T(8,128)(2,1)S(1)} all-gather(bf16[32,2048]{1,0:T(8,128)(2,1)S(1)} %convert_element_type.16), channel_id=1, replica_groups=mesh['groups'=2,'rows'=4,'sect'=4] {'sect'}, dimensions={1}, use_global_device_ids=true | all-gather | bytes 655360 | tf_op jit(solution)/shard_map/while/body/eval_jaxpr/all_gather | solution.py:46
  19.0 9.1 %collective-permute-done = bf16[32,8192]{1,0:T(8,128)(2,1)S(1)} collective-permute-done((bf16[32,8192]{1,0:T(8,128)(2,1)S(1)}, bf16[32,8192]{1,0:T(8,128)(2,1)S(1)}, u32[]{:S(2)}, u32[]{:S(2)}) %collective-permute-start) | collective-permute-done | bytes 524320 | tf_op jit(solution)/shard_map/while/body/eval_jaxpr/ppermute | solution.py:17
  29.9 6.0 %bitcast_reduce_fusion.2 = f32[32,8,256]{2,0,1:T(8,128)S(1)} fusion(bf16[64,256,256]{2,1,0:T(8,128)(2,1)} %get-tuple-element.121, bf16[64,32,256]{2,1,0:T(8,128)(2,1)S(1)} %gather_fusion, pred[64]{0:T(512)(128)(4,1)S(1)} %compare_and_fusion.2, bf16[64]{0:T(256)(128)(2,1)S(1)} %mul.60), kind=kOutput, calls=%fused_computation.2.clone.1 | convolution fusion | flops 269942784 | bytes 9699520 | tf_op jit(solution)/shard_map/while/body/eval_jaxpr/cqb,qab->cqa/dot_general | solution.py:50
  36.1 7.9 %all_gather.5 = bf16[32,8192]{1,0:T(8,128)(2,1)S(1)} all-gather(bf16[32,2048]{1,0:T(8,128)(2,1)S(1)} %convert_element_type.16), channel_id=1, replica_groups=mesh['groups'=2,'rows'=4,'sect'=4] {'sect'}, dimensions={1}, use_global_device_ids=true | all-gather | bytes 655360 | tf_op jit(solution)/shard_map/while/body/eval_jaxpr/all_gather | solution.py:46
  45.3 4.8 %collective-permute-start.1 = (bf16[32,8192]{1,0:T(8,128)(2,1)S(1)}, bf16[32,8192]{1,0:T(8,128)(2,1)S(1)}, u32[]{:S(2)}, u32[]{:S(2)}) collective-permute-start(bf16[32,8192]{1,0:T(8,128)(2,1)S(1)} %all_gather.5), channel_id=1, source_target_pairs={{0,4},{4,8},{8,12},{1,5},{5,9},{9,13},{2,6},{6,10},{10,14},{3,7},{... | collective-permute-start | bytes 1572872 | tf_op jit(solution)/shard_map/while/body/eval_jaxpr/ppermute | solution.py:16
  50.9 9.3 %collective-permute-done = bf16[32,8192]{1,0:T(8,128)(2,1)S(1)} collective-permute-done((bf16[32,8192]{1,0:T(8,128)(2,1)S(1)}, bf16[32,8192]{1,0:T(8,128)(2,1)S(1)}, u32[]{:S(2)}, u32[]{:S(2)}) %collective-permute-start) | collective-permute-done | bytes 524320 | tf_op jit(solution)/shard_map/while/body/eval_jaxpr/ppermute | solution.py:17
  62.1 6.0 %bitcast_reduce_fusion.2 = f32[32,8,256]{2,0,1:T(8,128)S(1)} fusion(bf16[64,256,256]{2,1,0:T(8,128)(2,1)} %get-tuple-element.121, bf16[64,32,256]{2,1,0:T(8,128)(2,1)S(1)} %gather_fusion, pred[64]{0:T(512)(128)(4,1)S(1)} %compare_and_fusion.2, bf16[64]{0:T(256)(128)(2,1)S(1)} %mul.60), kind=kOutput, calls=%fused_computation.2.clone.1 | convolution fusion | flops 269942784 | bytes 9699520 | tf_op jit(solution)/shard_map/while/body/eval_jaxpr/cqb,qab->cqa/dot_general | solution.py:50
  68.2 7.4 %all_gather.5 = bf16[32,8192]{1,0:T(8,128)(2,1)S(1)} all-gather(bf16[32,2048]{1,0:T(8,128)(2,1)S(1)} %convert_element_type.16), channel_id=1, replica_groups=mesh['groups'=2,'rows'=4,'sect'=4] {'sect'}, dimensions={1}, use_global_device_ids=true | all-gather | bytes 655360 | tf_op jit(solution)/shard_map/while/body/eval_jaxpr/all_gather | solution.py:46
  76.9 4.8 %collective-permute-start.1 = (bf16[32,8192]{1,0:T(8,128)(2,1)S(1)}, bf16[32,8192]{1,0:T(8,128)(2,1)S(1)}, u32[]{:S(2)}, u32[]{:S(2)}) collective-permute-start(bf16[32,8192]{1,0:T(8,128)(2,1)S(1)} %all_gather.5), channel_id=1, source_target_pairs={{0,4},{4,8},{8,12},{1,5},{5,9},{9,13},{2,6},{6,10},{10,14},{3,7},{... | collective-permute-start | bytes 1572872 | tf_op jit(solution)/shard_map/while/body/eval_jaxpr/ppermute | solution.py:16
  82.6 9.3 %collective-permute-done = bf16[32,8192]{1,0:T(8,128)(2,1)S(1)} collective-permute-done((bf16[32,8192]{1,0:T(8,128)(2,1)S(1)}, bf16[32,8192]{1,0:T(8,128)(2,1)S(1)}, u32[]{:S(2)}, u32[]{:S(2)}) %collective-permute-start) | collective-permute-done | bytes 524320 | tf_op jit(solution)/shard_map/while/body/eval_jaxpr/ppermute | solution.py:17
  93.8 6.0 %bitcast_reduce_fusion.2 = f32[32,8,256]{2,0,1:T(8,128)S(1)} fusion(bf16[64,256,256]{2,1,0:T(8,128)(2,1)} %get-tuple-element.121, bf16[64,32,256]{2,1,0:T(8,128)(2,1)S(1)} %gather_fusion, pred[64]{0:T(512)(128)(4,1)S(1)} %compare_and_fusion.2, bf16[64]{0:T(256)(128)(2,1)S(1)} %mul.60), kind=kOutput, calls=%fused_computation.2.clone.1 | convolution fusion | flops 269942784 | bytes 9699520 | tf_op jit(solution)/shard_map/while/body/eval_jaxpr/cqb,qab->cqa/dot_general | solution.py:50
  99.9 7.6 %all_gather.5 = bf16[32,8192]{1,0:T(8,128)(2,1)S(1)} all-gather(bf16[32,2048]{1,0:T(8,128)(2,1)S(1)} %convert_element_type.16), channel_id=1, replica_groups=mesh['groups'=2,'rows'=4,'sect'=4] {'sect'}, dimensions={1}, use_global_device_ids=true | all-gather | bytes 655360 | tf_op jit(solution)/shard_map/while/body/eval_jaxpr/all_gather | solution.py:46
  108.8 4.8 %collective-permute-start.1 = (bf16[32,8192]{1,0:T(8,128)(2,1)S(1)}, bf16[32,8192]{1,0:T(8,128)(2,1)S(1)}, u32[]{:S(2)}, u32[]{:S(2)}) collective-permute-start(bf16[32,8192]{1,0:T(8,128)(2,1)S(1)} %all_gather.5), channel_id=1, source_target_pairs={{0,4},{4,8},{8,12},{1,5},{5,9},{9,13},{2,6},{6,10},{10,14},{3,7},{... | collective-permute-start | bytes 1572872 | tf_op jit(solution)/shard_map/while/body/eval_jaxpr/ppermute | solution.py:16
  114.4 9.3 %collective-permute-done = bf16[32,8192]{1,0:T(8,128)(2,1)S(1)} collective-permute-done((bf16[32,8192]{1,0:T(8,128)(2,1)S(1)}, bf16[32,8192]{1,0:T(8,128)(2,1)S(1)}, u32[]{:S(2)}, u32[]{:S(2)}) %collective-permute-start) | collective-permute-done | bytes 524320 | tf_op jit(solution)/shard_map/while/body/eval_jaxpr/ppermute | solution.py:17
  125.6 6.0 %bitcast_reduce_fusion.2 = f32[32,8,256]{2,0,1:T(8,128)S(1)} fusion(bf16[64,256,256]{2,1,0:T(8,128)(2,1)} %get-tuple-element.121, bf16[64,32,256]{2,1,0:T(8,128)(2,1)S(1)} %gather_fusion, pred[64]{0:T(512)(128)(4,1)S(1)} %compare_and_fusion.2, bf16[64]{0:T(256)(128)(2,1)S(1)} %mul.60), kind=kOutput, calls=%fused_computation.2.clone.1 | convolution fusion | flops 269942784 | bytes 9699520 | tf_op jit(solution)/shard_map/while/body/eval_jaxpr/cqb,qab->cqa/dot_general | solution.py:50
  131.8 7.4 %all_gather.5 = bf16[32,8192]{1,0:T(8,128)(2,1)S(1)} all-gather(bf16[32,2048]{1,0:T(8,128)(2,1)S(1)} %convert_element_type.16), channel_id=1, replica_groups=mesh['groups'=2,'rows'=4,'sect'=4] {'sect'}, dimensions={1}, use_global_device_ids=true | all-gather | bytes 655360 | tf_op jit(solution)/shard_map/while/body/eval_jaxpr/all_gather | solution.py:46
  140.5 4.8 %collective-permute-start.1 = (bf16[32,8192]{1,0:T(8,128)(2,1)S(1)}, bf16[32,8192]{1,0:T(8,128)(2,1)S(1)}, u32[]{:S(2)}, u32[]{:S(2)}) collective-permute-start(bf16[32,8192]{1,0:T(8,128)(2,1)S(1)} %all_gather.5), channel_id=1, source_target_pairs={{0,4},{4,8},{8,12},{1,5},{5,9},{9,13},{2,6},{6,10},{10,14},{3,7},{... | collective-permute-start | bytes 1572872 | tf_op jit(solution)/shard_map/while/body/eval_jaxpr/ppermute | solution.py:16
  146.1 9.3 %collective-permute-done = bf16[32,8192]{1,0:T(8,128)(2,1)S(1)} collective-permute-done((bf16[32,8192]{1,0:T(8,128)(2,1)S(1)}, bf16[32,8192]{1,0:T(8,128)(2,1)S(1)}, u32[]{:S(2)}, u32[]{:S(2)}) %collective-permute-start) | collective-permute-done | bytes 524320 | tf_op jit(solution)/shard_map/while/body/eval_jaxpr/ppermute | solution.py:17
  157.3 6.0 %bitcast_reduce_fusion.2 = f32[32,8,256]{2,0,1:T(8,128)S(1)} fusion(bf16[64,256,256]{2,1,0:T(8,128)(2,1)} %get-tuple-element.121, bf16[64,32,256]{2,1,0:T(8,128)(2,1)S(1)} %gather_fusion, pred[64]{0:T(512)(128)(4,1)S(1)} %compare_and_fusion.2, bf16[64]{0:T(256)(128)(2,1)S(1)} %mul.60), kind=kOutput, calls=%fused_computation.2.clone.1 | convolution fusion | flops 269942784 | bytes 9699520 | tf_op jit(solution)/shard_map/while/body/eval_jaxpr/cqb,qab->cqa/dot_general | solution.py:50
  163.5 7.6 %all_gather.5 = bf16[32,8192]{1,0:T(8,128)(2,1)S(1)} all-gather(bf16[32,2048]{1,0:T(8,128)(2,1)S(1)} %convert_element_type.16), channel_id=1, replica_groups=mesh['groups'=2,'rows'=4,'sect'=4] {'sect'}, dimensions={1}, use_global_device_ids=true | all-gather | bytes 655360 | tf_op jit(solution)/shard_map/while/body/eval_jaxpr/all_gather | solution.py:46
  172.3 4.8 %collective-permute-start.1 = (bf16[32,8192]{1,0:T(8,128)(2,1)S(1)}, bf16[32,8192]{1,0:T(8,128)(2,1)S(1)}, u32[]{:S(2)}, u32[]{:S(2)}) collective-permute-start(bf16[32,8192]{1,0:T(8,128)(2,1)S(1)} %all_gather.5), channel_id=1, source_target_pairs={{0,4},{4,8},{8,12},{1,5},{5,9},{9,13},{2,6},{6,10},{10,14},{3,7},{... | collective-permute-start | bytes 1572872 | tf_op jit(solution)/shard_map/while/body/eval_jaxpr/ppermute | solution.py:16
  177.9 9.3 %collective-permute-done = bf16[32,8192]{1,0:T(8,128)(2,1)S(1)} collective-permute-done((bf16[32,8192]{1,0:T(8,128)(2,1)S(1)}, bf16[32,8192]{1,0:T(8,128)(2,1)S(1)}, u32[]{:S(2)}, u32[]{:S(2)}) %collective-permute-start) | collective-permute-done | bytes 524320 | tf_op jit(solution)/shard_map/while/body/eval_jaxpr/ppermute | solution.py:17
  189.2 6.0 %bitcast_reduce_fusion.2 = f32[32,8,256]{2,0,1:T(8,128)S(1)} fusion(bf16[64,256,256]{2,1,0:T(8,128)(2,1)} %get-tuple-element.121, bf16[64,32,256]{2,1,0:T(8,128)(2,1)S(1)} %gather_fusion, pred[64]{0:T(512)(128)(4,1)S(1)} %compare_and_fusion.2, bf16[64]{0:T(256)(128)(2,1)S(1)} %mul.60), kind=kOutput, calls=%fused_computation.2.clone.1 | convolution fusion | flops 269942784 | bytes 9699520 | tf_op jit(solution)/shard_map/while/body/eval_jaxpr/cqb,qab->cqa/dot_general | solution.py:50
  195.3 7.4 %all_gather.5 = bf16[32,8192]{1,0:T(8,128)(2,1)S(1)} all-gather(bf16[32,2048]{1,0:T(8,128)(2,1)S(1)} %convert_element_type.16), channel_id=1, replica_groups=mesh['groups'=2,'rows'=4,'sect'=4] {'sect'}, dimensions={1}, use_global_device_ids=true | all-gather | bytes 655360 | tf_op jit(solution)/shard_map/while/body/eval_jaxpr/all_gather | solution.py:46
  204.0 4.8 %collective-permute-start.1 = (bf16[32,8192]{1,0:T(8,128)(2,1)S(1)}, bf16[32,8192]{1,0:T(8,128)(2,1)S(1)}, u32[]{:S(2)}, u32[]{:S(2)}) collective-permute-start(bf16[32,8192]{1,0:T(8,128)(2,1)S(1)} %all_gather.5), channel_id=1, source_target_pairs={{0,4},{4,8},{8,12},{1,5},{5,9},{9,13},{2,6},{6,10},{10,14},{3,7},{... | collective-permute-start | bytes 1572872 | tf_op jit(solution)/shard_map/while/body/eval_jaxpr/ppermute | solution.py:16
  209.6 9.3 %collective-permute-done = bf16[32,8192]{1,0:T(8,128)(2,1)S(1)} collective-permute-done((bf16[32,8192]{1,0:T(8,128)(2,1)S(1)}, bf16[32,8192]{1,0:T(8,128)(2,1)S(1)}, u32[]{:S(2)}, u32[]{:S(2)}) %collective-permute-start) | collective-permute-done | bytes 524320 | tf_op jit(solution)/shard_map/while/body/eval_jaxpr/ppermute | solution.py:17
  220.9 6.0 %bitcast_reduce_fusion.2 = f32[32,8,256]{2,0,1:T(8,128)S(1)} fusion(bf16[64,256,256]{2,1,0:T(8,128)(2,1)} %get-tuple-element.121, bf16[64,32,256]{2,1,0:T(8,128)(2,1)S(1)} %gather_fusion, pred[64]{0:T(512)(128)(4,1)S(1)} %compare_and_fusion.2, bf16[64]{0:T(256)(128)(2,1)S(1)} %mul.60), kind=kOutput, calls=%fused_computation.2.clone.1 | convolution fusion | flops 269942784 | bytes 9699520 | tf_op jit(solution)/shard_map/while/body/eval_jaxpr/cqb,qab->cqa/dot_general | solution.py:50
  227.0 7.6 %all_gather.5 = bf16[32,8192]{1,0:T(8,128)(2,1)S(1)} all-gather(bf16[32,2048]{1,0:T(8,128)(2,1)S(1)} %convert_element_type.16), channel_id=1, replica_groups=mesh['groups'=2,'rows'=4,'sect'=4] {'sect'}, dimensions={1}, use_global_device_ids=true | all-gather | bytes 655360 | tf_op jit(solution)/shard_map/while/body/eval_jaxpr/all_gather | solution.py:46
  235.9 4.8 %collective-permute-start.1 = (bf16[32,8192]{1,0:T(8,128)(2,1)S(1)}, bf16[32,8192]{1,0:T(8,128)(2,1)S(1)}, u32[]{:S(2)}, u32[]{:S(2)}) collective-permute-start(bf16[32,8192]{1,0:T(8,128)(2,1)S(1)} %all_gather.5), channel_id=1, source_target_pairs={{0,4},{4,8},{8,12},{1,5},{5,9},{9,13},{2,6},{6,10},{10,14},{3,7},{... | collective-permute-start | bytes 1572872 | tf_op jit(solution)/shard_map/while/body/eval_jaxpr/ppermute | solution.py:16
  241.5 9.3 %collective-permute-done = bf16[32,8192]{1,0:T(8,128)(2,1)S(1)} collective-permute-done((bf16[32,8192]{1,0:T(8,128)(2,1)S(1)}, bf16[32,8192]{1,0:T(8,128)(2,1)S(1)}, u32[]{:S(2)}, u32[]{:S(2)}) %collective-permute-start) | collective-permute-done | bytes 524320 | tf_op jit(solution)/shard_map/while/body/eval_jaxpr/ppermute | solution.py:17
  252.7 6.0 %bitcast_reduce_fusion.2 = f32[32,8,256]{2,0,1:T(8,128)S(1)} fusion(bf16[64,256,256]{2,1,0:T(8,128)(2,1)} %get-tuple-element.121, bf16[64,32,256]{2,1,0:T(8,128)(2,1)S(1)} %gather_fusion, pred[64]{0:T(512)(128)(4,1)S(1)} %compare_and_fusion.2, bf16[64]{0:T(256)(128)(2,1)S(1)} %mul.60), kind=kOutput, calls=%fused_computation.2.clone.1 | convolution fusion | flops 269942784 | bytes 9699520 | tf_op jit(solution)/shard_map/while/body/eval_jaxpr/cqb,qab->cqa/dot_general | solution.py:50
  258.8 7.4 %all_gather.5 = bf16[32,8192]{1,0:T(8,128)(2,1)S(1)} all-gather(bf16[32,2048]{1,0:T(8,128)(2,1)S(1)} %convert_element_type.16), channel_id=1, replica_groups=mesh['groups'=2,'rows'=4,'sect'=4] {'sect'}, dimensions={1}, use_global_device_ids=true | all-gather | bytes 655360 | tf_op jit(solution)/shard_map/while/body/eval_jaxpr/all_gather | solution.py:46
  267.5 4.8 %collective-permute-start.1 = (bf16[32,8192]{1,0:T(8,128)(2,1)S(1)}, bf16[32,8192]{1,0:T(8,128)(2,1)S(1)}, u32[]{:S(2)}, u32[]{:S(2)}) collective-permute-start(bf16[32,8192]{1,0:T(8,128)(2,1)S(1)} %all_gather.5), channel_id=1, source_target_pairs={{0,4},{4,8},{8,12},{1,5},{5,9},{9,13},{2,6},{6,10},{10,14},{3,7},{... | collective-permute-start | bytes 1572872 | tf_op jit(solution)/shard_map/while/body/eval_jaxpr/ppermute | solution.py:16
  273.2 9.3 %collective-permute-done = bf16[32,8192]{1,0:T(8,128)(2,1)S(1)} collective-permute-done((bf16[32,8192]{1,0:T(8,128)(2,1)S(1)}, bf16[32,8192]{1,0:T(8,128)(2,1)S(1)}, u32[]{:S(2)}, u32[]{:S(2)}) %collective-permute-start) | collective-permute-done | bytes 524320 | tf_op jit(solution)/shard_map/while/body/eval_jaxpr/ppermute | solution.py:17
  284.4 6.0 %bitcast_reduce_fusion.2 = f32[32,8,256]{2,0,1:T(8,128)S(1)} fusion(bf16[64,256,256]{2,1,0:T(8,128)(2,1)} %get-tuple-element.121, bf16[64,32,256]{2,1,0:T(8,128)(2,1)S(1)} %gather_fusion, pred[64]{0:T(512)(128)(4,1)S(1)} %compare_and_fusion.2, bf16[64]{0:T(256)(128)(2,1)S(1)} %mul.60), kind=kOutput, calls=%fused_computation.2.clone.1 | convolution fusion | flops 269942784 | bytes 9699520 | tf_op jit(solution)/shard_map/while/body/eval_jaxpr/cqb,qab->cqa/dot_general | solution.py:50
  290.5 7.6 %all_gather.5 = bf16[32,8192]{1,0:T(8,128)(2,1)S(1)} all-gather(bf16[32,2048]{1,0:T(8,128)(2,1)S(1)} %convert_element_type.16), channel_id=1, replica_groups=mesh['groups'=2,'rows'=4,'sect'=4] {'sect'}, dimensions={1}, use_global_device_ids=true | all-gather | bytes 655360 | tf_op jit(solution)/shard_map/while/body/eval_jaxpr/all_gather | solution.py:46
  299.4 4.8 %collective-permute-start.1 = (bf16[32,8192]{1,0:T(8,128)(2,1)S(1)}, bf16[32,8192]{1,0:T(8,128)(2,1)S(1)}, u32[]{:S(2)}, u32[]{:S(2)}) collective-permute-start(bf16[32,8192]{1,0:T(8,128)(2,1)S(1)} %all_gather.5), channel_id=1, source_target_pairs={{0,4},{4,8},{8,12},{1,5},{5,9},{9,13},{2,6},{6,10},{10,14},{3,7},{... | collective-permute-start | bytes 1572872 | tf_op jit(solution)/shard_map/while/body/eval_jaxpr/ppermute | solution.py:16
  305.0 9.3 %collective-permute-done = bf16[32,8192]{1,0:T(8,128)(2,1)S(1)} collective-permute-done((bf16[32,8192]{1,0:T(8,128)(2,1)S(1)}, bf16[32,8192]{1,0:T(8,128)(2,1)S(1)}, u32[]{:S(2)}, u32[]{:S(2)}) %collective-permute-start) | collective-permute-done | bytes 524320 | tf_op jit(solution)/shard_map/while/body/eval_jaxpr/ppermute | solution.py:17
  316.2 6.0 %bitcast_reduce_fusion.2 = f32[32,8,256]{2,0,1:T(8,128)S(1)} fusion(bf16[64,256,256]{2,1,0:T(8,128)(2,1)} %get-tuple-element.121, bf16[64,32,256]{2,1,0:T(8,128)(2,1)S(1)} %gather_fusion, pred[64]{0:T(512)(128)(4,1)S(1)} %compare_and_fusion.2, bf16[64]{0:T(256)(128)(2,1)S(1)} %mul.60), kind=kOutput, calls=%fused_computation.2.clone.1 | convolution fusion | flops 269942784 | bytes 9699520 | tf_op jit(solution)/shard_map/while/body/eval_jaxpr/cqb,qab->cqa/dot_general | solution.py:50
  322.4 7.4 %all_gather.5 = bf16[32,8192]{1,0:T(8,128)(2,1)S(1)} all-gather(bf16[32,2048]{1,0:T(8,128)(2,1)S(1)} %convert_element_type.16), channel_id=1, replica_groups=mesh['groups'=2,'rows'=4,'sect'=4] {'sect'}, dimensions={1}, use_global_device_ids=true | all-gather | bytes 655360 | tf_op jit(solution)/shard_map/while/body/eval_jaxpr/all_gather | solution.py:46
  331.1 4.8 %collective-permute-start.1 = (bf16[32,8192]{1,0:T(8,128)(2,1)S(1)}, bf16[32,8192]{1,0:T(8,128)(2,1)S(1)}, u32[]{:S(2)}, u32[]{:S(2)}) collective-permute-start(bf16[32,8192]{1,0:T(8,128)(2,1)S(1)} %all_gather.5), channel_id=1, source_target_pairs={{0,4},{4,8},{8,12},{1,5},{5,9},{9,13},{2,6},{6,10},{10,14},{3,7},{... | collective-permute-start | bytes 1572872 | tf_op jit(solution)/shard_map/while/body/eval_jaxpr/ppermute | solution.py:16
  336.7 9.3 %collective-permute-done = bf16[32,8192]{1,0:T(8,128)(2,1)S(1)} collective-permute-done((bf16[32,8192]{1,0:T(8,128)(2,1)S(1)}, bf16[32,8192]{1,0:T(8,128)(2,1)S(1)}, u32[]{:S(2)}, u32[]{:S(2)}) %collective-permute-start) | collective-permute-done | bytes 524320 | tf_op jit(solution)/shard_map/while/body/eval_jaxpr/ppermute | solution.py:17
  347.9 6.0 %bitcast_reduce_fusion.2 = f32[32,8,256]{2,0,1:T(8,128)S(1)} fusion(bf16[64,256,256]{2,1,0:T(8,128)(2,1)} %get-tuple-element.121, bf16[64,32,256]{2,1,0:T(8,128)(2,1)S(1)} %gather_fusion, pred[64]{0:T(512)(128)(4,1)S(1)} %compare_and_fusion.2, bf16[64]{0:T(256)(128)(2,1)S(1)} %mul.60), kind=kOutput, calls=%fused_computation.2.clone.1 | convolution fusion | flops 269942784 | bytes 9699520 | tf_op jit(solution)/shard_map/while/body/eval_jaxpr/cqb,qab->cqa/dot_general | solution.py:50
  354.1 7.6 %all_gather.5 = bf16[32,8192]{1,0:T(8,128)(2,1)S(1)} all-gather(bf16[32,2048]{1,0:T(8,128)(2,1)S(1)} %convert_element_type.16), channel_id=1, replica_groups=mesh['groups'=2,'rows'=4,'sect'=4] {'sect'}, dimensions={1}, use_global_device_ids=true | all-gather | bytes 655360 | tf_op jit(solution)/shard_map/while/body/eval_jaxpr/all_gather | solution.py:46
  362.9 4.8 %collective-permute-start.1 = (bf16[32,8192]{1,0:T(8,128)(2,1)S(1)}, bf16[32,8192]{1,0:T(8,128)(2,1)S(1)}, u32[]{:S(2)}, u32[]{:S(2)}) collective-permute-start(bf16[32,8192]{1,0:T(8,128)(2,1)S(1)} %all_gather.5), channel_id=1, source_target_pairs={{0,4},{4,8},{8,12},{1,5},{5,9},{9,13},{2,6},{6,10},{10,14},{3,7},{... | collective-permute-start | bytes 1572872 | tf_op jit(solution)/shard_map/while/body/eval_jaxpr/ppermute | solution.py:16
  368.6 9.3 %collective-permute-done = bf16[32,8192]{1,0:T(8,128)(2,1)S(1)} collective-permute-done((bf16[32,8192]{1,0:T(8,128)(2,1)S(1)}, bf16[32,8192]{1,0:T(8,128)(2,1)S(1)}, u32[]{:S(2)}, u32[]{:S(2)}) %collective-permute-start) | collective-permute-done | bytes 524320 | tf_op jit(solution)/shard_map/while/body/eval_jaxpr/ppermute | solution.py:17
  379.8 6.0 %bitcast_reduce_fusion.2 = f32[32,8,256]{2,0,1:T(8,128)S(1)} fusion(bf16[64,256,256]{2,1,0:T(8,128)(2,1)} %get-tuple-element.121, bf16[64,32,256]{2,1,0:T(8,128)(2,1)S(1)} %gather_fusion, pred[64]{0:T(512)(128)(4,1)S(1)} %compare_and_fusion.2, bf16[64]{0:T(256)(128)(2,1)S(1)} %mul.60), kind=kOutput, calls=%fused_computation.2.clone.1 | convolution fusion | flops 269942784 | bytes 9699520 | tf_op jit(solution)/shard_map/while/body/eval_jaxpr/cqb,qab->cqa/dot_general | solution.py:50
  (163 shorter events, 57.3 us)
Async XLA Ops:
  12.9 15.3 %collective-permute-start = (bf16[32,8192]{1,0:T(8,128)(2,1)S(1)}, bf16[32,8192]{1,0:T(8,128)(2,1)S(1)}, u32[]{:S(2)}, u32[]{:S(2)}) collective-permute-start(bf16[32,8192]{1,0:T(8,128)(2,1)S(1)} %all_gather.5), channel_id=1, source_target_pairs={{4,0},{8,4},{12,8},{5,1},{9,5},{13,9},{6,2},{10,6},{14,10},{7,3},{... | collective-permute-start | bytes 1572872 | tf_op jit(solution)/shard_map/while/body/eval_jaxpr/ppermute | solution.py:17
  14.1 14.8 %collective-permute-start.1 = (bf16[32,8192]{1,0:T(8,128)(2,1)S(1)}, bf16[32,8192]{1,0:T(8,128)(2,1)S(1)}, u32[]{:S(2)}, u32[]{:S(2)}) collective-permute-start(bf16[32,8192]{1,0:T(8,128)(2,1)S(1)} %all_gather.5), channel_id=1, source_target_pairs={{0,4},{4,8},{8,12},{1,5},{5,9},{9,13},{2,6},{6,10},{10,14},{3,7},{... | collective-permute-start | bytes 1572872 | tf_op jit(solution)/shard_map/while/body/eval_jaxpr/ppermute | solution.py:16
  44.0 16.2 %collective-permute-start = (bf16[32,8192]{1,0:T(8,128)(2,1)S(1)}, bf16[32,8192]{1,0:T(8,128)(2,1)S(1)}, u32[]{:S(2)}, u32[]{:S(2)}) collective-permute-start(bf16[32,8192]{1,0:T(8,128)(2,1)S(1)} %all_gather.5), channel_id=1, source_target_pairs={{4,0},{8,4},{12,8},{5,1},{9,5},{13,9},{6,2},{10,6},{14,10},{7,3},{... | collective-permute-start | bytes 1572872 | tf_op jit(solution)/shard_map/while/body/eval_jaxpr/ppermute | solution.py:17
  45.3 15.9 %collective-permute-start.1 = (bf16[32,8192]{1,0:T(8,128)(2,1)S(1)}, bf16[32,8192]{1,0:T(8,128)(2,1)S(1)}, u32[]{:S(2)}, u32[]{:S(2)}) collective-permute-start(bf16[32,8192]{1,0:T(8,128)(2,1)S(1)} %all_gather.5), channel_id=1, source_target_pairs={{0,4},{4,8},{8,12},{1,5},{5,9},{9,13},{2,6},{6,10},{10,14},{3,7},{... | collective-permute-start | bytes 1572872 | tf_op jit(solution)/shard_map/while/body/eval_jaxpr/ppermute | solution.py:16
  75.6 16.2 %collective-permute-start = (bf16[32,8192]{1,0:T(8,128)(2,1)S(1)}, bf16[32,8192]{1,0:T(8,128)(2,1)S(1)}, u32[]{:S(2)}, u32[]{:S(2)}) collective-permute-start(bf16[32,8192]{1,0:T(8,128)(2,1)S(1)} %all_gather.5), channel_id=1, source_target_pairs={{4,0},{8,4},{12,8},{5,1},{9,5},{13,9},{6,2},{10,6},{14,10},{7,3},{... | collective-permute-start | bytes 1572872 | tf_op jit(solution)/shard_map/while/body/eval_jaxpr/ppermute | solution.py:17
  76.9 15.9 %collective-permute-start.1 = (bf16[32,8192]{1,0:T(8,128)(2,1)S(1)}, bf16[32,8192]{1,0:T(8,128)(2,1)S(1)}, u32[]{:S(2)}, u32[]{:S(2)}) collective-permute-start(bf16[32,8192]{1,0:T(8,128)(2,1)S(1)} %all_gather.5), channel_id=1, source_target_pairs={{0,4},{4,8},{8,12},{1,5},{5,9},{9,13},{2,6},{6,10},{10,14},{3,7},{... | collective-permute-start | bytes 1572872 | tf_op jit(solution)/shard_map/while/body/eval_jaxpr/ppermute | solution.py:16
  107.5 16.2 %collective-permute-start = (bf16[32,8192]{1,0:T(8,128)(2,1)S(1)}, bf16[32,8192]{1,0:T(8,128)(2,1)S(1)}, u32[]{:S(2)}, u32[]{:S(2)}) collective-permute-start(bf16[32,8192]{1,0:T(8,128)(2,1)S(1)} %all_gather.5), channel_id=1, source_target_pairs={{4,0},{8,4},{12,8},{5,1},{9,5},{13,9},{6,2},{10,6},{14,10},{7,3},{... | collective-permute-start | bytes 1572872 | tf_op jit(solution)/shard_map/while/body/eval_jaxpr/ppermute | solution.py:17
  108.8 15.9 %collective-permute-start.1 = (bf16[32,8192]{1,0:T(8,128)(2,1)S(1)}, bf16[32,8192]{1,0:T(8,128)(2,1)S(1)}, u32[]{:S(2)}, u32[]{:S(2)}) collective-permute-start(bf16[32,8192]{1,0:T(8,128)(2,1)S(1)} %all_gather.5), channel_id=1, source_target_pairs={{0,4},{4,8},{8,12},{1,5},{5,9},{9,13},{2,6},{6,10},{10,14},{3,7},{... | collective-permute-start | bytes 1572872 | tf_op jit(solution)/shard_map/while/body/eval_jaxpr/ppermute | solution.py:16
  139.2 16.2 %collective-permute-start = (bf16[32,8192]{1,0:T(8,128)(2,1)S(1)}, bf16[32,8192]{1,0:T(8,128)(2,1)S(1)}, u32[]{:S(2)}, u32[]{:S(2)}) collective-permute-start(bf16[32,8192]{1,0:T(8,128)(2,1)S(1)} %all_gather.5), channel_id=1, source_target_pairs={{4,0},{8,4},{12,8},{5,1},{9,5},{13,9},{6,2},{10,6},{14,10},{7,3},{... | collective-permute-start | bytes 1572872 | tf_op jit(solution)/shard_map/while/body/eval_jaxpr/ppermute | solution.py:17
  140.5 15.9 %collective-permute-start.1 = (bf16[32,8192]{1,0:T(8,128)(2,1)S(1)}, bf16[32,8192]{1,0:T(8,128)(2,1)S(1)}, u32[]{:S(2)}, u32[]{:S(2)}) collective-permute-start(bf16[32,8192]{1,0:T(8,128)(2,1)S(1)} %all_gather.5), channel_id=1, source_target_pairs={{0,4},{4,8},{8,12},{1,5},{5,9},{9,13},{2,6},{6,10},{10,14},{3,7},{... | collective-permute-start | bytes 1572872 | tf_op jit(solution)/shard_map/while/body/eval_jaxpr/ppermute | solution.py:16
  171.0 16.2 %collective-permute-start = (bf16[32,8192]{1,0:T(8,128)(2,1)S(1)}, bf16[32,8192]{1,0:T(8,128)(2,1)S(1)}, u32[]{:S(2)}, u32[]{:S(2)}) collective-permute-start(bf16[32,8192]{1,0:T(8,128)(2,1)S(1)} %all_gather.5), channel_id=1, source_target_pairs={{4,0},{8,4},{12,8},{5,1},{9,5},{13,9},{6,2},{10,6},{14,10},{7,3},{... | collective-permute-start | bytes 1572872 | tf_op jit(solution)/shard_map/while/body/eval_jaxpr/ppermute | solution.py:17
  172.3 15.9 %collective-permute-start.1 = (bf16[32,8192]{1,0:T(8,128)(2,1)S(1)}, bf16[32,8192]{1,0:T(8,128)(2,1)S(1)}, u32[]{:S(2)}, u32[]{:S(2)}) collective-permute-start(bf16[32,8192]{1,0:T(8,128)(2,1)S(1)} %all_gather.5), channel_id=1, source_target_pairs={{0,4},{4,8},{8,12},{1,5},{5,9},{9,13},{2,6},{6,10},{10,14},{3,7},{... | collective-permute-start | bytes 1572872 | tf_op jit(solution)/shard_map/while/body/eval_jaxpr/ppermute | solution.py:16
  202.7 16.2 %collective-permute-start = (bf16[32,8192]{1,0:T(8,128)(2,1)S(1)}, bf16[32,8192]{1,0:T(8,128)(2,1)S(1)}, u32[]{:S(2)}, u32[]{:S(2)}) collective-permute-start(bf16[32,8192]{1,0:T(8,128)(2,1)S(1)} %all_gather.5), channel_id=1, source_target_pairs={{4,0},{8,4},{12,8},{5,1},{9,5},{13,9},{6,2},{10,6},{14,10},{7,3},{... | collective-permute-start | bytes 1572872 | tf_op jit(solution)/shard_map/while/body/eval_jaxpr/ppermute | solution.py:17
  204.0 15.9 %collective-permute-start.1 = (bf16[32,8192]{1,0:T(8,128)(2,1)S(1)}, bf16[32,8192]{1,0:T(8,128)(2,1)S(1)}, u32[]{:S(2)}, u32[]{:S(2)}) collective-permute-start(bf16[32,8192]{1,0:T(8,128)(2,1)S(1)} %all_gather.5), channel_id=1, source_target_pairs={{0,4},{4,8},{8,12},{1,5},{5,9},{9,13},{2,6},{6,10},{10,14},{3,7},{... | collective-permute-start | bytes 1572872 | tf_op jit(solution)/shard_map/while/body/eval_jaxpr/ppermute | solution.py:16
  234.6 16.2 %collective-permute-start = (bf16[32,8192]{1,0:T(8,128)(2,1)S(1)}, bf16[32,8192]{1,0:T(8,128)(2,1)S(1)}, u32[]{:S(2)}, u32[]{:S(2)}) collective-permute-start(bf16[32,8192]{1,0:T(8,128)(2,1)S(1)} %all_gather.5), channel_id=1, source_target_pairs={{4,0},{8,4},{12,8},{5,1},{9,5},{13,9},{6,2},{10,6},{14,10},{7,3},{... | collective-permute-start | bytes 1572872 | tf_op jit(solution)/shard_map/while/body/eval_jaxpr/ppermute | solution.py:17
  235.9 15.9 %collective-permute-start.1 = (bf16[32,8192]{1,0:T(8,128)(2,1)S(1)}, bf16[32,8192]{1,0:T(8,128)(2,1)S(1)}, u32[]{:S(2)}, u32[]{:S(2)}) collective-permute-start(bf16[32,8192]{1,0:T(8,128)(2,1)S(1)} %all_gather.5), channel_id=1, source_target_pairs={{0,4},{4,8},{8,12},{1,5},{5,9},{9,13},{2,6},{6,10},{10,14},{3,7},{... | collective-permute-start | bytes 1572872 | tf_op jit(solution)/shard_map/while/body/eval_jaxpr/ppermute | solution.py:16
  266.3 16.2 %collective-permute-start = (bf16[32,8192]{1,0:T(8,128)(2,1)S(1)}, bf16[32,8192]{1,0:T(8,128)(2,1)S(1)}, u32[]{:S(2)}, u32[]{:S(2)}) collective-permute-start(bf16[32,8192]{1,0:T(8,128)(2,1)S(1)} %all_gather.5), channel_id=1, source_target_pairs={{4,0},{8,4},{12,8},{5,1},{9,5},{13,9},{6,2},{10,6},{14,10},{7,3},{... | collective-permute-start | bytes 1572872 | tf_op jit(solution)/shard_map/while/body/eval_jaxpr/ppermute | solution.py:17
  267.5 15.9 %collective-permute-start.1 = (bf16[32,8192]{1,0:T(8,128)(2,1)S(1)}, bf16[32,8192]{1,0:T(8,128)(2,1)S(1)}, u32[]{:S(2)}, u32[]{:S(2)}) collective-permute-start(bf16[32,8192]{1,0:T(8,128)(2,1)S(1)} %all_gather.5), channel_id=1, source_target_pairs={{0,4},{4,8},{8,12},{1,5},{5,9},{9,13},{2,6},{6,10},{10,14},{3,7},{... | collective-permute-start | bytes 1572872 | tf_op jit(solution)/shard_map/while/body/eval_jaxpr/ppermute | solution.py:16
  298.1 16.2 %collective-permute-start = (bf16[32,8192]{1,0:T(8,128)(2,1)S(1)}, bf16[32,8192]{1,0:T(8,128)(2,1)S(1)}, u32[]{:S(2)}, u32[]{:S(2)}) collective-permute-start(bf16[32,8192]{1,0:T(8,128)(2,1)S(1)} %all_gather.5), channel_id=1, source_target_pairs={{4,0},{8,4},{12,8},{5,1},{9,5},{13,9},{6,2},{10,6},{14,10},{7,3},{... | collective-permute-start | bytes 1572872 | tf_op jit(solution)/shard_map/while/body/eval_jaxpr/ppermute | solution.py:17
  299.4 15.9 %collective-permute-start.1 = (bf16[32,8192]{1,0:T(8,128)(2,1)S(1)}, bf16[32,8192]{1,0:T(8,128)(2,1)S(1)}, u32[]{:S(2)}, u32[]{:S(2)}) collective-permute-start(bf16[32,8192]{1,0:T(8,128)(2,1)S(1)} %all_gather.5), channel_id=1, source_target_pairs={{0,4},{4,8},{8,12},{1,5},{5,9},{9,13},{2,6},{6,10},{10,14},{3,7},{... | collective-permute-start | bytes 1572872 | tf_op jit(solution)/shard_map/while/body/eval_jaxpr/ppermute | solution.py:16
  329.8 16.2 %collective-permute-start = (bf16[32,8192]{1,0:T(8,128)(2,1)S(1)}, bf16[32,8192]{1,0:T(8,128)(2,1)S(1)}, u32[]{:S(2)}, u32[]{:S(2)}) collective-permute-start(bf16[32,8192]{1,0:T(8,128)(2,1)S(1)} %all_gather.5), channel_id=1, source_target_pairs={{4,0},{8,4},{12,8},{5,1},{9,5},{13,9},{6,2},{10,6},{14,10},{7,3},{... | collective-permute-start | bytes 1572872 | tf_op jit(solution)/shard_map/while/body/eval_jaxpr/ppermute | solution.py:17
  331.1 15.9 %collective-permute-start.1 = (bf16[32,8192]{1,0:T(8,128)(2,1)S(1)}, bf16[32,8192]{1,0:T(8,128)(2,1)S(1)}, u32[]{:S(2)}, u32[]{:S(2)}) collective-permute-start(bf16[32,8192]{1,0:T(8,128)(2,1)S(1)} %all_gather.5), channel_id=1, source_target_pairs={{0,4},{4,8},{8,12},{1,5},{5,9},{9,13},{2,6},{6,10},{10,14},{3,7},{... | collective-permute-start | bytes 1572872 | tf_op jit(solution)/shard_map/while/body/eval_jaxpr/ppermute | solution.py:16
  361.6 16.2 %collective-permute-start = (bf16[32,8192]{1,0:T(8,128)(2,1)S(1)}, bf16[32,8192]{1,0:T(8,128)(2,1)S(1)}, u32[]{:S(2)}, u32[]{:S(2)}) collective-permute-start(bf16[32,8192]{1,0:T(8,128)(2,1)S(1)} %all_gather.5), channel_id=1, source_target_pairs={{4,0},{8,4},{12,8},{5,1},{9,5},{13,9},{6,2},{10,6},{14,10},{7,3},{... | collective-permute-start | bytes 1572872 | tf_op jit(solution)/shard_map/while/body/eval_jaxpr/ppermute | solution.py:17
  362.9 15.9 %collective-permute-start.1 = (bf16[32,8192]{1,0:T(8,128)(2,1)S(1)}, bf16[32,8192]{1,0:T(8,128)(2,1)S(1)}, u32[]{:S(2)}, u32[]{:S(2)}) collective-permute-start(bf16[32,8192]{1,0:T(8,128)(2,1)S(1)} %all_gather.5), channel_id=1, source_target_pairs={{0,4},{4,8},{8,12},{1,5},{5,9},{9,13},{2,6},{6,10},{10,14},{3,7},{... | collective-permute-start | bytes 1572872 | tf_op jit(solution)/shard_map/while/body/eval_jaxpr/ppermute | solution.py:16
  385.9 0.7 copy-start
where the time goes:
time: 389 us; the launch traced here: 387 us
  waiting for transfers between devices  123 us (32%)
  blocking collectives  91.3 us (23%)
  starting transfers between devices  71.9 us (18%)
  matrix products  71.6 us (18%)
  local copies, waits for them, and re-layouts  14.2 us (4%)
  other arithmetic  12.2 us (3%)
    ppermute x12, waiting for transfers between devices, padded(): after = lax.ppermute(first, axis, down)  112 us
    all_gather x12, blocking collectives, advance(): pieces = lax.all_gather(narrow, 'sect', axis=1, tiled=True)  91.3 us
    dot_general x12, matrix products, advance(): jnp.einsum('cqb,qab->cqa', chosen, flat_blocks, preferred_element_type=jn...  71.6 us
    ppermute x12, starting transfers between devices, padded(): before = lax.ppermute(last, axis, up)  56.5 us
    ppermute x12, starting transfers between devices, padded(): after = lax.ppermute(first, axis, down)  15.4 us
    ppermute x12, waiting for transfers between devices, padded(): before = lax.ppermute(last, axis, up)  11.4 us
    convert_element_type x12, other arithmetic, per_device(): live = (jnp.arange(slots, dtype=jnp.int32)[None, :] < counts[:, None]).as...  8.74 us
  transfers between devices with their start and end apart: 24, of which 24 were waited for; matrix products, arithmetic and copies ran while one was open for 3% of the time, Pallas kernels for 0%

commit v1 on v0

v1 whole, which is shorter than its diff:
```python
import functools

import jax
import jax.numpy as jnp
from jax import lax
from jax.experimental import pallas as pl
from jax.experimental.pallas import tpu as pltpu
from jax.sharding import PartitionSpec as P

STEPS = 12
CHUNKS = 2
VIA_ROWS = 5
KINDS = 15


def kernel(
    ranges,
    sections,
    slots,
    col_ref,
    counts_ref,
    shifts_ref,
    blocks_hbm,
    vec_ref,
    out_ref,
    blocks_ref,
    *scratch,
):
    windows = [scratch[2 * h : 2 * h + 2] for h in range(CHUNKS)]
    send_sem, recv_sem, load_sem = scratch[2 * CHUNKS :]
    rblk, _, width, _ = blocks_ref.shape
    ncols = vec_ref.shape[0]
    cols = ncols // CHUNKS
    z = lax.axis_index("rows")
    s = lax.axis_index("sect")
    partner = s + 1 - 2 * lax.rem(s, 2)
    across = lax.rem(s + 2, sections)
    has_below = z > 0
    has_above = z < ranges - 1
    stretch = sections * rblk
    zero_block = 3 * stretch
    base = (z - 1) * stretch
    via_rows = rblk * VIA_ROWS // 8

    loads = [
        pltpu.make_async_copy(blocks_hbm.at[k], blocks_ref.at[k], load_sem.at[k])
        for k in range(rblk)
    ]
    for load in loads:
        load.start()

    barrier = pltpu.get_barrier_semaphore()

    def greet(**device):
        pl.semaphore_signal(
            barrier, inc=1, device_id=device, device_id_type=pl.DeviceIdType.MESH
        )

    greet(sect=partner)
    greet(sect=across)
    pl.when(has_above)(lambda: greet(rows=z + 1))
    pl.when(has_below)(lambda: greet(rows=z - 1))

    shift = jnp.where(s == 0, shifts_ref[0], shifts_ref[1])

    whole = (0, rblk)
    upper = (0, via_rows)
    lower = (via_rows, rblk - via_rows)
    always = None
    to_partner = {"sect": partner}
    to_across = {"sect": across}
    to_above = {"rows": z + 1}
    to_below = {"rows": z - 1}
    table = {
        0: (always, always, to_partner, (1, s), whole, 1, (1, partner)),
        1: (always, always, to_across, (1, s), whole, 1, (1, across)),
        2: (has_above, has_below, to_above, (1, s), whole, 0, (0, s)),
        3: (has_below, has_above, to_below, (1, s), whole, 2, (2, s)),
        4: (always, always, to_partner, (1, across), whole, 1, (1, lax.rem(partner + 2, sections))),
        5: (has_above, has_below, to_above, (1, across), upper, 0, (0, across)),
        6: (has_below, has_above, to_below, (1, across), upper, 2, (2, across)),
        7: (has_below, has_below, to_partner, (0, s), whole, 0, (0, partner)),
        8: (has_above, has_above, to_partner, (2, s), whole, 2, (2, partner)),
        9: (has_below, has_below, to_across, (0, s), lower, 0, (0, across)),
        10: (has_above, has_above, to_across, (2, s), lower, 2, (2, across)),
        11: (has_below, has_below, to_partner, (0, across), upper, 0, (0, lax.rem(partner + 2, sections))),
        12: (has_above, has_above, to_partner, (2, across), upper, 2, (2, lax.rem(partner + 2, sections))),
        13: (has_below, has_below, to_partner, (0, across), lower, 0, (0, lax.rem(partner + 2, sections))),
        14: (has_above, has_above, to_partner, (2, across), lower, 2, (2, lax.rem(partner + 2, sections))),
    }

    def region(window, place, part):
        span, section = place
        first, count = part
        return window.at[pl.ds((span * sections + section) * rblk + first, count)]

    def guarded(condition, action):
        if condition is None:
            action()
        else:
            pl.when(condition)(action)

    def outgoing(h, par, kind):
        _, _, device, source, part, landing, _ = table[kind]
        window = windows[h][par]
        return pltpu.make_async_remote_copy(
            src_ref=region(window, source, part),
            dst_ref=region(window, (landing, source[1]), part),
            send_sem=send_sem.at[h, par, kind],
            recv_sem=recv_sem.at[h, par, kind],
            device_id=device,
            device_id_type=pl.DeviceIdType.MESH,
        )

    def send(h, par, *kinds):
        for kind in kinds:
            guarded(table[kind][0], lambda kind=kind: outgoing(h, par, kind).start())

    def sent(h, par):
        for kind in range(KINDS):
            guarded(table[kind][0], lambda kind=kind: outgoing(h, par, kind).wait_send())

    def received(h, par, *kinds):
        for kind in kinds:
            _, condition, device, _, part, _, place = table[kind]
            window = windows[h][par]

            def wait(kind=kind, place=place, part=part, device=device, window=window):
                pltpu.make_async_remote_copy(
                    src_ref=region(window, place, part),
                    dst_ref=region(window, place, part),
                    send_sem=send_sem.at[h, par, kind],
                    recv_sem=recv_sem.at[h, par, kind],
                    device_id=device,
                    device_id_type=pl.DeviceIdType.MESH,
                ).wait_recv()

            guarded(condition, wait)

    def relay_first(h, par):
        received(h, par, 1)
        send(h, par, 5, 6, 4)
        received(h, par, 2)
        send(h, par, 9, 7)
        received(h, par, 3)
        send(h, par, 10, 8)

    def relay_second(h, par):
        received(h, par, 5)
        send(h, par, 11)
        received(h, par, 6)
        send(h, par, 12)
        received(h, par, 9)
        send(h, par, 13)
        received(h, par, 10)
        send(h, par, 14)

    def gathered(h, par):
        received(h, par, 0, 4, 7, 8, 11, 12, 13, 14)

    def rows_of(h):
        return pl.ds(h * cols, cols)

    def apply_row(h, par, k):
        window = windows[h][par]
        here = pl.ds(pl.multiple_of(k * width, width), width)
        total = shift * out_ref[rows_of(h), here]
        for j in range(slots):
            position = jnp.where(j < counts_ref[k], col_ref[k, j] - base, zero_block)
            total += lax.dot_general(
                window[position],
                blocks_ref[k, j],
                (((1,), (1,)), ((), ())),
                preferred_element_type=jnp.float32,
            )
        out_ref[rows_of(h), here] = total
        windows[h][1 - par][stretch + s * rblk + k] = total.astype(jnp.bfloat16)

    def apply_rows(h, par, first, count):
        def body(k, carry):
            apply_row(h, par, k)
            return carry

        lax.fori_loop(first, first + count, body, 0, unroll=True)

    out_ref[...] = vec_ref[...]
    for h in range(CHUNKS):
        for par in range(2):
            windows[h][par][zero_block] = jnp.zeros((cols, width), jnp.bfloat16)
        for k in range(rblk):
            windows[h][0][stretch + s * rblk + k] = vec_ref[
                rows_of(h), pl.ds(k * width, width)
            ].astype(jnp.bfloat16)

    neighbours = 2 + has_below.astype(jnp.int32) + has_above.astype(jnp.int32)
    pl.semaphore_wait(barrier, neighbours)
    for h in range(CHUNKS):
        send(h, 0, 1, 2, 3, 0)
    for load in loads:
        load.wait()
    relay_first(0, 0)
    relay_second(0, 0)

    half = rblk // 2

    def two_steps(i, carry):
        for par in range(2):
            more = None if par == 0 else i < STEPS // 2 - 1
            for h in range(CHUNKS):
                last = h == CHUNKS - 1
                other, other_par = (0, 1 - par) if last else (h + 1, par)
                other_runs = more if last else None
                gathered(h, par)
                if CHUNKS > 1:
                    apply_rows(h, par, 0, half // 2)
                    guarded(other_runs, lambda: relay_first(other, other_par))
                    apply_rows(h, par, half // 2, rblk - half // 2 - half // 2)
                    guarded(other_runs, lambda: relay_second(other, other_par))
                    apply_rows(h, par, rblk - half // 2, half // 2)
                else:
                    apply_rows(h, par, 0, rblk)
                sent(h, par)
                guarded(more, lambda: send(h, 1 - par, 1, 2, 3, 0))
                if CHUNKS == 1:
                    guarded(more, lambda: relay_first(h, 1 - par))
                    guarded(more, lambda: relay_second(h, 1 - par))
        return carry

    lax.fori_loop(0, STEPS // 2, two_steps, 0)


def per_device(ranges, sections, blocks, col_index, counts, shifts, vectors):
    rblk, slots, width, _ = blocks.shape
    ncols = vectors.shape[0]
    window = pltpu.VMEM((3 * sections * rblk + 1, ncols // CHUNKS, width), jnp.bfloat16)
    smem = pl.BlockSpec(memory_space=pltpu.SMEM)
    vmem = pl.BlockSpec(memory_space=pltpu.VMEM)
    return pl.pallas_call(
        functools.partial(kernel, ranges, sections, slots),
        out_shape=jax.ShapeDtypeStruct(vectors.shape, jnp.float32),
        in_specs=[smem, smem, smem, pl.BlockSpec(memory_space=pl.ANY), vmem],
        out_specs=vmem,
        scratch_shapes=[
            pltpu.VMEM(blocks.shape, jnp.bfloat16),
            *[window] * (2 * CHUNKS),
            pltpu.SemaphoreType.DMA((CHUNKS, 2, KINDS)),
            pltpu.SemaphoreType.DMA((CHUNKS, 2, KINDS)),
            pltpu.SemaphoreType.DMA((rblk,)),
        ],
        compiler_params=pltpu.CompilerParams(
            collective_id=0, has_side_effects=True, vmem_limit_bytes=40 * 2**20
        ),
        cost_estimate=pl.CostEstimate(
            flops=2 * STEPS * ncols * blocks.size,
            bytes_accessed=2 * blocks.size + 8 * vectors.size,
            transcendentals=0,
        ),
    )(col_index, counts, shifts, blocks, vectors)


def solution(mesh):
    return jax.shard_map(
        functools.partial(per_device, mesh.shape["rows"], mesh.shape["sect"]),
        mesh=mesh,
        in_specs=(
            P(("rows", "sect"), None, None, None),
            P(("rows", "sect"), None),
            P(("rows", "sect")),
            P("groups"),
            P("groups", ("rows", "sect")),
        ),
        out_specs=P("groups", ("rows", "sect")),
        check_vma=False,
    )
```

time: 389 us -> 197 us (0.51)
  Pallas kernels: 0 us -> 190 us
  waiting for transfers between devices: 123 us -> 0 us
  blocking collectives: 91.3 us -> 0 us
  starting transfers between devices: 71.9 us -> 0 us
  matrix products: 71.6 us -> 0 us
  other arithmetic: 12.2 us -> 0 us
  local copies, waits for them, and re-layouts: 14.2 us -> 7.03 us
    pallas_call x0 -> x1, Pallas kernels: none -> 190 us  [per_device(): pl.pallas_call(functools.partial(kernel, ranges, sections, slots), out_sh...]
    ppermute x24 -> x0, waiting for transfers between devices: 123 us -> none  [the longest x12 112 us: padded(): after = lax.ppermute(first, axis, down)]
    all_gather x12 -> x0, blocking collectives: 91.3 us -> none  [advance(): pieces = lax.all_gather(narrow, 'sect', axis=1, tiled=True)]
    ppermute x24 -> x0, starting transfers between devices: 71.9 us -> none  [the longest x12 56.5 us: padded(): before = lax.ppermute(last, axis, up)]
    dot_general x12 -> x0, matrix products: 71.6 us -> none  [advance(): jnp.einsum('cqb,qab->cqa', chosen, flat_blocks, preferred_element_type=jn...]
    convert_element_type x24 -> x0, other arithmetic: 8.94 us -> none  [the longest x12 8.74 us: per_device(): live = (jnp.arange(slots, dtype=jnp.int32)[None, :] < counts[:, None]).as...]
    gather x12 -> x0, local copies, waits for them, and re-layouts: 7.45 us -> none  [advance(): chosen = jnp.take(window, position, axis=1) * live[None, :, None]]
    unnamed x3 -> x11, local copies, waits for them, and re-layouts: 1.65 us -> 7.03 us
  transfers between devices with their start and end apart: 24 -> 0, of which waited for: 24 -> 0; matrix products, arithmetic and copies ran while one was open for 3% -> 0% of each run, Pallas kernels for 0% -> 0%
where the time goes in v1:
time: 197 us
  Pallas kernels  190 us (96%)
  local copies, waits for them, and re-layouts  7.03 us (4%)
    pallas_call x1, Pallas kernels, per_device(): pl.pallas_call(functools.partial(kernel, ranges, sections, slots), out_sh...  190 us
    unnamed x11, local copies, waits for them, and re-layouts  7.03 us

profile of v1, /device:TPU:1, one launch (start us, length us, event | category | flops | bytes accessed | tf_op | source)
XLA Modules:
  0.0 196.7 jit_solution(7566605245613429374)
XLA Ops:
  0.0 0.0 copy-start
  0.0 3.4 %copy-done = bf16[8,8,256,256]{3,2,1,0:T(8,128)(2,1)S(1)} copy-done((bf16[8,8,256,256]{3,2,1,0:T(8,128)(2,1)S(1)}, bf16[8,8,256,256]{3,2,1,0:T(8,128)(2,1)}, u32[]{:S(2)}) %copy-start) | copy-done | bytes 8388632
  3.4 0.0 copy-start.1
  3.4 0.9 copy-done.1
  4.3 0.0 copy-start.2
  4.3 0.7 copy-done.2
  5.0 0.0 copy-start.3
  5.0 0.7 copy-done.3
  5.7 0.0 copy-start.4
  5.7 0.7 copy-done.4
  6.3 189.7 %shard_map.55 = f32[32,2048]{1,0:T(8,128)S(1)} custom-call(s32[8,8]{1,0:T(8,128)S(1)} %copy-done.2, s32[8]{0:T(128)S(1)} %copy-done.3, f32[2]{0:T(128)S(1)} %copy-done.4, bf16[8,8,256,256]{3,2,1,0:T(8,128)(2,1)S(1)} %copy-done, f32[32,2048]{1,0:T(8,128)S(1)} %copy-done.1), custom_call_target="tpu_custom_call" | custom-call | flops 3221225472 | bytes 8912896 | tf_op jit(solution)/shard_map/pallas_call | solution.py:238
  196.0 0.7 copy.7
Async XLA Ops:
  0.0 3.4 %copy-start = (bf16[8,8,256,256]{3,2,1,0:T(8,128)(2,1)S(1)}, bf16[8,8,256,256]{3,2,1,0:T(8,128)(2,1)}, u32[]{:S(2)}) copy-start(bf16[8,8,256,256]{3,2,1,0:T(8,128)(2,1)} %blocks_hbm.1) | copy-start | bytes 25165828
  3.4 0.9 copy-start.1
  4.3 0.7 copy-start.2
  5.0 0.7 copy-start.3
  5.7 0.7 copy-start.4

commit v2 on v1

v2 whole, which is shorter than its diff:
```python
import functools

import jax
import jax.numpy as jnp
from jax import lax
from jax.experimental import pallas as pl
from jax.experimental.pallas import tpu as pltpu
from jax.sharding import PartitionSpec as P

STEPS = 12
KINDS = 13
GROUPS = 4
VIA_ROWS = (0, 2, 3)


def kernel(
    ranges,
    sections,
    slots,
    col_ref,
    counts_ref,
    shifts_ref,
    blocks_hbm,
    vec_ref,
    out_ref,
    blocks_ref,
    *scratch,
):
    windows = scratch[:2]
    send_sem, recv_sem, load_sem = scratch[2:]
    rblk, _, width, _ = blocks_ref.shape
    ncols = vec_ref.shape[0]
    count = rblk // GROUPS
    z = lax.axis_index("rows")
    s = lax.axis_index("sect")
    partner = s + 1 - 2 * lax.rem(s, 2)
    across = lax.rem(s + 2, sections)
    has_below = z > 0
    has_above = z < ranges - 1
    stretch = sections * rblk
    zero_block = 3 * stretch
    base = (z - 1) * stretch

    loads = [
        pltpu.make_async_copy(blocks_hbm.at[k], blocks_ref.at[k], load_sem.at[k])
        for k in range(rblk)
    ]
    for load in loads:
        load.start()

    barrier = pltpu.get_barrier_semaphore()

    def greet(**device):
        pl.semaphore_signal(
            barrier, inc=1, device_id=device, device_id_type=pl.DeviceIdType.MESH
        )

    greet(sect=partner)
    greet(sect=across)
    pl.when(has_above)(lambda: greet(rows=z + 1))
    pl.when(has_below)(lambda: greet(rows=z - 1))

    shift = jnp.where(s == 0, shifts_ref[0], shifts_ref[1])

    always = None
    diagonal = lax.rem(partner + 2, sections)
    to_partner = {"sect": partner}
    to_across = {"sect": across}
    to_above = {"rows": z + 1}
    to_below = {"rows": z - 1}
    table = (
        (always, always, to_partner, (1, s), 1, (1, partner)),
        (always, always, to_across, (1, s), 1, (1, across)),
        (has_above, has_below, to_above, (1, s), 0, (0, s)),
        (has_below, has_above, to_below, (1, s), 2, (2, s)),
        (always, always, to_partner, (1, across), 1, (1, diagonal)),
        (has_above, has_below, to_above, (1, across), 0, (0, across)),
        (has_below, has_above, to_below, (1, across), 2, (2, across)),
        (has_below, has_below, to_partner, (0, s), 0, (0, partner)),
        (has_above, has_above, to_partner, (2, s), 2, (2, partner)),
        (has_below, has_below, to_across, (0, s), 0, (0, across)),
        (has_above, has_above, to_across, (2, s), 2, (2, across)),
        (has_below, has_below, to_partner, (0, across), 0, (0, diagonal)),
        (has_above, has_above, to_partner, (2, across), 2, (2, diagonal)),
    )

    def region(par, span, section, g):
        return windows[par].at[pl.ds((span * sections + section) * rblk + g * count, count)]

    def guarded(condition, action):
        if condition is None:
            action()
        else:
            pl.when(condition)(action)

    def copy(par, kind, g, source, target):
        return pltpu.make_async_remote_copy(
            src_ref=source,
            dst_ref=target,
            send_sem=send_sem.at[par, kind, g],
            recv_sem=recv_sem.at[par, kind, g],
            device_id=table[kind][2],
            device_id_type=pl.DeviceIdType.MESH,
        )

    def outgoing(par, kind, g):
        _, _, _, (span, section), landing, _ = table[kind]
        return copy(par, kind, g, region(par, span, section, g), region(par, landing, section, g))

    def send(par, g, *kinds):
        for kind in kinds:
            guarded(table[kind][0], lambda kind=kind: outgoing(par, kind, g).start())

    def sent(par):
        for kind in range(KINDS):
            for g in range(GROUPS):
                if kind in (5, 6) and g not in VIA_ROWS or kind in (9, 10) and g in VIA_ROWS:
                    continue
                guarded(table[kind][0], lambda: outgoing(par, kind, g).wait_send())

    def received(par, g, *kinds):
        for kind in kinds:
            landed = region(par, *table[kind][5], g)
            guarded(
                table[kind][1], lambda: copy(par, kind, g, landed, landed).wait_recv()
            )

    def relay(par):
        for g in range(GROUPS):
            received(par, g, 1)
            if g in VIA_ROWS:
                send(par, g, 5, 6)
            send(par, g, 4)
            for kind, along, beside in ((2, 9, 7), (3, 10, 8)):
                received(par, g, kind)
                if g not in VIA_ROWS:
                    send(par, g, along)
                send(par, g, beside)
        for g in range(GROUPS):
            for kind, beside in zip((5, 6) if g in VIA_ROWS else (9, 10), (11, 12)):
                received(par, g, kind)
                send(par, g, beside)

    def gathered(par):
        for g in range(GROUPS):
            received(par, g, 0, 4, 7, 8, 11, 12)

    own = stretch + s * rblk

    def place(k):
        return pl.ds(k * width, width)

    def product(x, k, j):
        return lax.dot_general(
            x, blocks_ref[k, j], (((1,), (1,)), ((), ())), preferred_element_type=jnp.float32
        )

    def apply_self(par):
        for k in range(rblk):
            out_ref[:, place(k)] = shift * out_ref[:, place(k)] + product(
                windows[par][own + k], k, 0
            )

    def apply_others(par, k):
        total = out_ref[:, place(k)]
        for j in range(1, slots):
            position = jnp.where(j < counts_ref[k], col_ref[k, j] - base, zero_block)
            total += product(windows[par][position], k, j)
        out_ref[:, place(k)] = total
        windows[1 - par][own + k] = total.astype(jnp.bfloat16)

    out_ref[...] = vec_ref[...]
    for par in range(2):
        windows[par][zero_block] = jnp.zeros((ncols, width), jnp.bfloat16)
    for k in range(rblk):
        windows[0][own + k] = vec_ref[:, place(k)].astype(jnp.bfloat16)

    neighbours = 2 + has_below.astype(jnp.int32) + has_above.astype(jnp.int32)
    pl.semaphore_wait(barrier, neighbours)
    for g in range(GROUPS):
        send(0, g, 1, 2, 3, 0)
    relay(0)
    for load in loads:
        load.wait()
    apply_self(0)

    def two_steps(i, carry):
        for par in range(2):
            more = None if par == 0 else i < STEPS // 2 - 1
            gathered(par)
            for g in range(GROUPS):
                for k in range(g * count, (g + 1) * count):
                    apply_others(par, k)
                if g == GROUPS - 1:
                    sent(par)
                guarded(more, lambda: send(1 - par, g, 1, 2, 3, 0))
            guarded(more, lambda: apply_self(1 - par))
            guarded(more, lambda: relay(1 - par))
        return carry

    lax.fori_loop(0, STEPS // 2, two_steps, 0)


def per_device(ranges, sections, blocks, col_index, counts, shifts, vectors):
    rblk, slots, width, _ = blocks.shape
    ncols = vectors.shape[0]
    window = pltpu.VMEM((3 * sections * rblk + 1, ncols, width), jnp.bfloat16)
    smem = pl.BlockSpec(memory_space=pltpu.SMEM)
    vmem = pl.BlockSpec(memory_space=pltpu.VMEM)
    return pl.pallas_call(
        functools.partial(kernel, ranges, sections, slots),
        out_shape=jax.ShapeDtypeStruct(vectors.shape, jnp.float32),
        in_specs=[smem, smem, smem, pl.BlockSpec(memory_space=pl.ANY), vmem],
        out_specs=vmem,
        scratch_shapes=[
            pltpu.VMEM(blocks.shape, jnp.bfloat16),
            window,
            window,
            pltpu.SemaphoreType.DMA((2, KINDS, GROUPS)),
            pltpu.SemaphoreType.DMA((2, KINDS, GROUPS)),
            pltpu.SemaphoreType.DMA((rblk,)),
        ],
        compiler_params=pltpu.CompilerParams(
            collective_id=0, has_side_effects=True, vmem_limit_bytes=40 * 2**20
        ),
        cost_estimate=pl.CostEstimate(
            flops=2 * STEPS * ncols * blocks.size,
            bytes_accessed=2 * blocks.size + 8 * vectors.size,
            transcendentals=0,
        ),
    )(col_index, counts, shifts, blocks, vectors)


def solution(mesh):
    return jax.shard_map(
        functools.partial(per_device, mesh.shape["rows"], mesh.shape["sect"]),
        mesh=mesh,
        in_specs=(
            P(("rows", "sect"), None, None, None),
            P(("rows", "sect"), None),
            P(("rows", "sect")),
            P("groups"),
            P("groups", ("rows", "sect")),
        ),
        out_specs=P("groups", ("rows", "sect")),
        check_vma=False,
    )
```

time: 197 us -> 128 us (0.65)
  Pallas kernels: 190 us -> 121 us
    pallas_call x1, Pallas kernels: 190 us -> 121 us  [per_device(): pl.pallas_call(functools.partial(kernel, ranges, sections, slots), out_sh...]
where the time goes in v2:
time: 128 us
  Pallas kernels  121 us (95%)
  local copies, waits for them, and re-layouts  7.03 us (5%)
    pallas_call x1, Pallas kernels, per_device(): pl.pallas_call(functools.partial(kernel, ranges, sections, slots), out_sh...  121 us
    unnamed x11, local copies, waits for them, and re-layouts  7.03 us

profile of v2, /device:TPU:1, one launch (start us, length us, event | category | flops | bytes accessed | tf_op | source)
XLA Modules:
  0.0 128.1 jit_solution(16244272866184807896)
XLA Ops:
  0.0 0.0 copy-start
  0.0 3.4 %copy-done = bf16[8,8,256,256]{3,2,1,0:T(8,128)(2,1)S(1)} copy-done((bf16[8,8,256,256]{3,2,1,0:T(8,128)(2,1)S(1)}, bf16[8,8,256,256]{3,2,1,0:T(8,128)(2,1)}, u32[]{:S(2)}) %copy-start) | copy-done | bytes 8388632
  3.4 0.0 copy-start.1
  3.4 0.9 copy-done.1
  4.3 0.0 copy-start.2
  4.3 0.7 copy-done.2
  5.0 0.0 copy-start.3
  5.0 0.7 copy-done.3
  5.7 0.0 copy-start.4
  5.7 0.7 copy-done.4
  6.3 121.0 %shard_map.55 = f32[32,2048]{1,0:T(8,128)S(1)} custom-call(s32[8,8]{1,0:T(8,128)S(1)} %copy-done.2, s32[8]{0:T(128)S(1)} %copy-done.3, f32[2]{0:T(128)S(1)} %copy-done.4, bf16[8,8,256,256]{3,2,1,0:T(8,128)(2,1)S(1)} %copy-done, f32[32,2048]{1,0:T(8,128)S(1)} %copy-done.1), custom_call_target="tpu_custom_call" | custom-call | flops 3221225472 | bytes 8912896 | tf_op jit(solution)/shard_map/pallas_call | solution.py:210
  127.4 0.7 copy.7
Async XLA Ops:
  0.0 3.4 %copy-start = (bf16[8,8,256,256]{3,2,1,0:T(8,128)(2,1)S(1)}, bf16[8,8,256,256]{3,2,1,0:T(8,128)(2,1)}, u32[]{:S(2)}) copy-start(bf16[8,8,256,256]{3,2,1,0:T(8,128)(2,1)} %blocks_hbm.1) | copy-start | bytes 25165828
  3.4 0.9 copy-start.1
  4.3 0.7 copy-start.2
  5.0 0.7 copy-start.3
  5.7 0.7 copy-start.4

commit v3 on v2

--- a/solution.py
+++ b/solution.py
@@ -8,9 +8,11 @@
 from jax.sharding import PartitionSpec as P
 
 STEPS = 12
-KINDS = 13
-GROUPS = 4
-VIA_ROWS = (0, 2, 3)
+KINDS = 15
+ROUTES = "rrrr"
+EIGHTHS = (2, 2, 2, 2)
+GROUPS = len(ROUTES)
+RELAYED = {"r": (5, 6), "s": (9, 10), "d": (13, 14)}
 
 
 def kernel(
@@ -27,10 +29,10 @@
     *scratch,
 ):
     windows = scratch[:2]
-    send_sem, recv_sem, load_sem = scratch[2:]
+    send_sem, recv_sem, partner_sem, load_sem = scratch[2:]
     rblk, _, width, _ = blocks_ref.shape
     ncols = vec_ref.shape[0]
-    count = rblk // GROUPS
+    edges = [rblk * sum(EIGHTHS[:g]) // 8 for g in range(GROUPS + 1)]
     z = lax.axis_index("rows")
     s = lax.axis_index("sect")
     partner = s + 1 - 2 * lax.rem(s, 2)
@@ -57,8 +59,16 @@
 
     greet(sect=partner)
     greet(sect=across)
-    pl.when(has_above)(lambda: greet(rows=z + 1))
-    pl.when(has_below)(lambda: greet(rows=z - 1))
+
+    @pl.when(has_above)
+    def _():
+        greet(rows=z + 1)
+        greet(rows=z + 1, sect=across)
+
+    @pl.when(has_below)
+    def _():
+        greet(rows=z - 1)
+        greet(rows=z - 1, sect=across)
 
     shift = jnp.where(s == 0, shifts_ref[0], shifts_ref[1])
 
@@ -82,10 +92,14 @@
         (has_above, has_above, to_across, (2, s), 2, (2, across)),
         (has_below, has_below, to_partner, (0, across), 0, (0, diagonal)),
         (has_above, has_above, to_partner, (2, across), 2, (2, diagonal)),
+        (has_above, has_below, {"rows": z + 1, "sect": across}, (1, s), 0, (0, across)),
+        (has_below, has_above, {"rows": z - 1, "sect": across}, (1, s), 2, (2, across)),
     )
+    send_class = (0, 0, 1, 2, 0, 1, 2, 2, 1, 2, 1, 2, 1, 1, 2)
+    partner_class = {0: 0, 4: 0, 7: 1, 11: 1, 8: 2, 12: 2}
 
     def region(par, span, section, g):
-        return windows[par].at[pl.ds((span * sections + section) * rblk + g * count, count)]
+        return windows[par].at[pl.ds((span * sections + section) * rblk + edges[g], edges[g + 1] - edges[g])]
 
     def guarded(condition, action):
         if condition is None:
@@ -97,8 +111,10 @@
         return pltpu.make_async_remote_copy(
             src_ref=source,
             dst_ref=target,
-            send_sem=send_sem.at[par, kind, g],
-            recv_sem=recv_sem.at[par, kind, g],
+            send_sem=send_sem.at[par, send_class[kind]],
+            recv_sem=partner_sem.at[par, partner_class[kind]]
+            if kind in partner_class
+            else recv_sem.at[par, kind, g],
             device_id=table[kind][2],
             device_id_type=pl.DeviceIdType.MESH,
         )
@@ -112,11 +128,9 @@
             guarded(table[kind][0], lambda kind=kind: outgoing(par, kind, g).start())
 
     def sent(par):
-        for kind in range(KINDS):
-            for g in range(GROUPS):
-                if kind in (5, 6) and g not in VIA_ROWS or kind in (9, 10) and g in VIA_ROWS:
-                    continue
-                guarded(table[kind][0], lambda: outgoing(par, kind, g).wait_send())
+        for kind, pieces in ((0, 3), (2, 4), (3, 4)):
+            everything = windows[par].at[pl.ds(0, pieces * rblk)]
+            guarded(table[kind][0], lambda: copy(par, kind, 0, everything, everything).wait_send())
 
     def received(par, g, *kinds):
         for kind in kinds:
@@ -125,25 +139,36 @@
                 table[kind][1], lambda: copy(par, kind, g, landed, landed).wait_recv()
             )
 
+    def start(par, g):
+        send(par, g, 1, 2, 3, 0)
+        if ROUTES[g] == "d":
+            send(par, g, 13, 14)
+
     def relay(par):
         for g in range(GROUPS):
             received(par, g, 1)
-            if g in VIA_ROWS:
+            if ROUTES[g] == "r":
                 send(par, g, 5, 6)
+            if ROUTES[g] == "s":
+                received(par, g, 2)
+                send(par, g, 9)
+                received(par, g, 3)
+                send(par, g, 10)
+        for g in range(GROUPS):
             send(par, g, 4)
-            for kind, along, beside in ((2, 9, 7), (3, 10, 8)):
-                received(par, g, kind)
-                if g not in VIA_ROWS:
-                    send(par, g, along)
+            for kind, beside in ((2, 7), (3, 8)):
+                if ROUTES[g] != "s":
+                    received(par, g, kind)
                 send(par, g, beside)
         for g in range(GROUPS):
-            for kind, beside in zip((5, 6) if g in VIA_ROWS else (9, 10), (11, 12)):
+            for kind, beside in zip(RELAYED[ROUTES[g]], (11, 12)):
                 received(par, g, kind)
                 send(par, g, beside)
 
     def gathered(par):
-        for g in range(GROUPS):
-            received(par, g, 0, 4, 7, 8, 11, 12)
+        for kind in (0, 7, 8):
+            both = windows[par].at[pl.ds(0, 2 * rblk)]
+            guarded(table[kind][1], lambda: copy(par, kind, 0, both, both).wait_recv())
 
     own = stretch + s * rblk
 
@@ -175,10 +200,10 @@
     for k in range(rblk):
         windows[0][own + k] = vec_ref[:, place(k)].astype(jnp.bfloat16)
 
-    neighbours = 2 + has_below.astype(jnp.int32) + has_above.astype(jnp.int32)
+    neighbours = 2 + 2 * (has_below.astype(jnp.int32) + has_above.astype(jnp.int32))
     pl.semaphore_wait(barrier, neighbours)
     for g in range(GROUPS):
-        send(0, g, 1, 2, 3, 0)
+        start(0, g)
     relay(0)
     for load in loads:
         load.wait()
@@ -189,11 +214,11 @@
             more = None if par == 0 else i < STEPS // 2 - 1
             gathered(par)
             for g in range(GROUPS):
-                for k in range(g * count, (g + 1) * count):
+                for k in range(edges[g], edges[g + 1]):
                     apply_others(par, k)
                 if g == GROUPS - 1:
                     sent(par)
-                guarded(more, lambda: send(1 - par, g, 1, 2, 3, 0))
+                guarded(more, lambda: start(1 - par, g))
             guarded(more, lambda: apply_self(1 - par))
             guarded(more, lambda: relay(1 - par))
         return carry
@@ -216,8 +241,9 @@
             pltpu.VMEM(blocks.shape, jnp.bfloat16),
             window,
             window,
+            pltpu.SemaphoreType.DMA((2, 3)),
             pltpu.SemaphoreType.DMA((2, KINDS, GROUPS)),
-            pltpu.SemaphoreType.DMA((2, KINDS, GROUPS)),
+            pltpu.SemaphoreType.DMA((2, 3)),
             pltpu.SemaphoreType.DMA((rblk,)),
         ],
         compiler_params=pltpu.CompilerParams(

time: 128 us -> 128 us (level)
  no operation moved by 1% of the time
where the time goes in v3:
time: 128 us
  Pallas kernels  121 us (95%)
  local copies, waits for them, and re-layouts  7.03 us (5%)
    pallas_call x1, Pallas kernels, per_device(): pl.pallas_call(functools.partial(kernel, ranges, sections, slots), out_sh...  121 us
    unnamed x11, local copies, waits for them, and re-layouts  7.03 us

profile of v3, /device:TPU:1, one launch (start us, length us, event | category | flops | bytes accessed | tf_op | source)
XLA Modules:
  0.0 128.2 jit_solution(10716868142730818549)
XLA Ops:
  0.0 0.0 copy-start
  0.0 3.4 %copy-done = bf16[8,8,256,256]{3,2,1,0:T(8,128)(2,1)S(1)} copy-done((bf16[8,8,256,256]{3,2,1,0:T(8,128)(2,1)S(1)}, bf16[8,8,256,256]{3,2,1,0:T(8,128)(2,1)}, u32[]{:S(2)}) %copy-start) | copy-done | bytes 8388632
  3.4 0.0 copy-start.1
  3.4 0.9 copy-done.1
  4.3 0.0 copy-start.2
  4.3 0.7 copy-done.2
  5.0 0.0 copy-start.3
  5.0 0.7 copy-done.3
  5.7 0.0 copy-start.4
  5.7 0.7 copy-done.4
  6.3 121.2 %shard_map.55 = f32[32,2048]{1,0:T(8,128)S(1)} custom-call(s32[8,8]{1,0:T(8,128)S(1)} %copy-done.2, s32[8]{0:T(128)S(1)} %copy-done.3, f32[2]{0:T(128)S(1)} %copy-done.4, bf16[8,8,256,256]{3,2,1,0:T(8,128)(2,1)S(1)} %copy-done, f32[32,2048]{1,0:T(8,128)S(1)} %copy-done.1), custom_call_target="tpu_custom_call" | custom-call | flops 3221225472 | bytes 8912896 | tf_op jit(solution)/shard_map/pallas_call | solution.py:235
  127.5 0.7 copy.7
Async XLA Ops:
  0.0 3.4 %copy-start = (bf16[8,8,256,256]{3,2,1,0:T(8,128)(2,1)S(1)}, bf16[8,8,256,256]{3,2,1,0:T(8,128)(2,1)}, u32[]{:S(2)}) copy-start(bf16[8,8,256,256]{3,2,1,0:T(8,128)(2,1)} %blocks_hbm.1) | copy-start | bytes 25165828
  3.4 0.9 copy-start.1
  4.3 0.7 copy-start.2
  5.0 0.7 copy-start.3
  5.7 0.7 copy-start.4
